TPU v7x, 32 devices: a whole 2x2x4 slice. The times are simulated.
32 devices in a mesh: groups: 2 (over y), tp: 4 (over z), dp: 4 (over x, core).
Axes of the slice: x: 2, y: 2, z: 4, core: 2. Of those that a mesh axis runs over, the one named last changes fastest.
Arguments:
- queries: bfloat16 [8, 128, 1024], P(('groups', 'dp'), None, 'tp'), parts along dimension 0, may hold values from -90 to 90
- cache: bfloat16 [8, 4, 2, 3584, 128], P(('groups', 'dp'), 'tp'), parts along dimension 0, may hold values from -4.5 to 4.5
- new_kv: bfloat16 [8, 4, 2, 128, 128], P(('groups', 'dp'), 'tp'), parts along dimension 0, may hold values from -4.5 to 4.5
- out_weight: bfloat16 [1024, 4096], P('tp'), may hold values from -0.25 to 0.25
- prefix: int32 [8], P(('groups', 'dp')), parts along dimension 0, may hold values from 896 to 3584, as said below
Outputs:
- mixed: bfloat16 [8, 128, 4096], P(('groups', 'dp')), parts along dimension 0
There are 2 independent parts, one for each index of `groups`. A program takes and returns all parts, laid end to end along the dimension named above; an argument that names none is the same for every part. Nothing has to cross between parts.
Inputs may be any that keep to these rules, and one draw needn't show every extreme that they name: `prefix`: the largest entry is 3584 in every draw.
All inputs are finite; a program needn't handle non-finite values. Where the computation divides by a largest or mean magnitude, that divisor is 1e-20 or more.
Results may differ from a plain program's by a relative error of at most 0.014.
Values may be sent and summed in bfloat16 or wider, within the bound.
A program may use at most 64 MiB of HBM per device.

v0:
```python
import jax
import jax.numpy as jnp
from jax import lax
from jax.sharding import PartitionSpec as P

DW = 4096
HD = 128
HQ_DEV = 2
BLOCK = 128
CH = 128
PMAX = 3584


def encode(values):
    blocks = values.reshape(values.shape[:-1] + (values.shape[-1] // BLOCK, BLOCK))
    scales = (jnp.max(jnp.abs(blocks), axis=-1) + 1e-06).astype(jnp.bfloat16)
    encoded = (blocks / scales.astype(jnp.float32)[..., None]).astype(jnp.bfloat16)
    encoded, scales = lax.optimization_barrier((encoded, scales))
    return (encoded.reshape(values.shape), scales)


def decode(encoded, scales):
    blocks = encoded.reshape(encoded.shape[:-1] + (encoded.shape[-1] // BLOCK, BLOCK)).astype(
        jnp.float32
    )
    return (blocks * scales.astype(jnp.float32)[..., None]).reshape(encoded.shape)


def attend(query_rows, past_kv, fresh_kv, length):
    factor = HD ** (-0.5)
    query_heads = query_rows.reshape(CH, HQ_DEV, HD)
    past_scores = (
        jnp.einsum("ckd,pd->kcp", query_heads, past_kv[0], preferred_element_type=jnp.float32)
        * factor
    )
    fresh_scores = (
        jnp.einsum("ckd,jd->kcj", query_heads, fresh_kv[0], preferred_element_type=jnp.float32)
        * factor
    )
    visible = jnp.arange(PMAX) < length
    causal = jnp.arange(CH)[None, :] <= jnp.arange(CH)[:, None]
    past_scores = jnp.where(visible, past_scores, -jnp.inf)
    fresh_scores = jnp.where(causal, fresh_scores, -jnp.inf)
    highest = jnp.maximum(jnp.max(past_scores, axis=-1), jnp.max(fresh_scores, axis=-1))[..., None]
    past_weights = jnp.exp(past_scores - highest)
    fresh_weights = jnp.exp(fresh_scores - highest)
    totals = jnp.sum(past_weights, axis=-1) + jnp.sum(fresh_weights, axis=-1)
    summed = jnp.einsum(
        "kcp,pd->ckd",
        past_weights.astype(jnp.bfloat16),
        past_kv[1],
        preferred_element_type=jnp.float32,
    )
    summed = summed + jnp.einsum(
        "kcj,jd->ckd",
        fresh_weights.astype(jnp.bfloat16),
        fresh_kv[1],
        preferred_element_type=jnp.float32,
    )
    attended = summed / jnp.transpose(totals, (1, 0))[..., None]
    return attended.astype(jnp.bfloat16).reshape(CH, HQ_DEV * HD)


def per_device(queries, cache, new_kv, out_weight, prefix):
    attended = attend(queries[0], cache[0, 0], new_kv[0, 0], prefix[0])
    partial_value = jnp.dot(attended, out_weight, preferred_element_type=jnp.float32)
    encoded, scales = encode(partial_value)
    ranks = lax.axis_size("tp")
    outgoing = (
        encoded.reshape(CH, ranks, DW // ranks),
        scales.reshape(CH, ranks, DW // BLOCK // ranks),
    )
    code_piece = lax.all_to_all(outgoing[0], "tp", split_axis=1, concat_axis=1, tiled=True)
    scale_piece = lax.all_to_all(outgoing[1], "tp", split_axis=1, concat_axis=1, tiled=True)
    recoded, rescales = encode(jnp.sum(decode(code_piece, scale_piece), axis=1))
    recoded, rescales = (
        lax.all_gather(recoded, "tp", axis=1, tiled=True),
        lax.all_gather(rescales, "tp", axis=1, tiled=True),
    )
    mixed = decode(recoded, rescales).astype(jnp.bfloat16)
    return mixed[None]


def solution(mesh):
    in_specs = (
        P(("groups", "dp"), None, "tp"),
        P(("groups", "dp"), "tp", None, None, None),
        P(("groups", "dp"), "tp", None, None, None),
        P("tp", None),
        P(("groups", "dp")),
    )
    out_specs = P(("groups", "dp"), None, None)
    return jax.shard_map(
        per_device, mesh=mesh, in_specs=in_specs, out_specs=out_specs, check_vma=False
    )
```

profile of v0, /device:TPU:0, one launch (start us, length us, event | category | flops | bytes accessed | tf_op | source)
XLA Modules:
  0.0 97.6 jit_solution(5954221198122860349)
XLA Ops:
  6.6 0.9 reshape_squeeze.3
  8.1 0.0 copy-start.2
  8.1 3.3 %fusion.31 = (f32[2,128]{1,0:T(2,128)S(1)}, f32[2,128,3584]{1,2,0:T(8,128)S(1)}) fusion(bf16[128,2,128]{2,1,0:T(2,128)(2,1)S(1)} %reshape_squeeze.3, bf16[1,1,2,3584,128]{4,3,2,1,0:T(8,128)(2,1)} %param.6, pred[3584]{0:T(1024)(128)(4,1)S(1)} %iota_compare_fusion.1), kind=kOutput, calls=%fused_computation.45 | convolution fusion | flops 237633280 | bytes 4657664 | tf_op jit(solution)/shard_map/ckd,pd->kcp/dot_general | solution.py:33
  11.4 0.0 copy-done.2
  11.4 0.0 copy-start.1
  11.4 0.2 fusion.32
  11.6 0.5 fusion.2
  12.1 0.8 copy-done.1
  12.9 0.6 fusion.6
  13.6 3.3 %copy.28 = bf16[4096,256]{1,0:T(8,128)(2,1)S(1)} copy(bf16[4096,256]{0,1:T(8,128)(2,1)} %bitcast.70) | data formatting | bytes 4194304 | tf_op jit(solution)/shard_map/dot_general | solution.py:66
  16.9 0.2 fusion.13
  17.1 0.7 abs_reduce_fusion
  17.9 1.2 %divide_convert_fusion = bf16[128,32,128]{0,2,1:T(8,128)(2,1)} fusion(f32[128,32,128]{0,2,1:T(8,128)S(1)} %get-tuple-element.22, f32[128,32]{0,1:T(8,128)S(1)} %get-tuple-element.15), kind=kLoop, calls=%fused_computation.10 | loop fusion | flops 1048576 | bytes 3162112 | tf_op jit(solution)/shard_map/convert_element_type | solution.py:17
  19.1 11.7 %all_to_all.10 = bf16[128,4,8]{0,2,1:T(8,128)(2,1)S(1)} all-to-all(bf16[128,4,8]{0,2,1:T(8,128)(2,1)S(1)} %bitcast.73), channel_id=1, replica_groups=mesh['groups'=2,'tp'=4,'dp'=4] {'tp'}, dimensions={1} | all-to-all | bytes 16384 | tf_op jit(solution)/shard_map/all_to_all | solution.py:74
  30.8 3.5 %all-to-all-start = ((bf16[128,4,1024]{0,2,1:T(8,128)(2,1)}), bf16[128,4,1024]{0,2,1:T(8,128)(2,1)S(1)}, u32[]{:S(2)}, u32[]{:S(2)}) async-start(bf16[128,4,1024]{0,2,1:T(8,128)(2,1)} %bitcast.17), calls=%async_computation | async-start | bytes 2097152 | tf_op jit(solution)/shard_map/all_to_all | solution.py:73
  34.3 0.0 all-gather.2.cloned.1.call-start
  34.4 24.5 %all-to-all-done = bf16[128,4,1024]{0,2,1:T(8,128)(2,1)S(1)} async-done(((bf16[128,4,1024]{0,2,1:T(8,128)(2,1)}), bf16[128,4,1024]{0,2,1:T(8,128)(2,1)S(1)}, u32[]{:S(2)}, u32[]{:S(2)}) %all-to-all-start) | async-done | bytes 1048608 | tf_op jit(solution)/shard_map/all_to_all | solution.py:73
  58.9 0.2 fusion.5
  59.2 0.1 divide_convert_fusion.1
  59.2 0.9 copy.29
  60.1 0.0 all-gather.2.cloned.1.call-update
  60.1 11.9 %all_gather.7 = bf16[128,32]{0,1:T(8,128)(2,1)S(1)} all-gather(bf16[128,8]{0,1:T(8,128)(2,1)S(1)} %get-tuple-element.12), channel_id=1, replica_groups=mesh['groups'=2,'tp'=4,'dp'=4] {'tp'}, dimensions={1}, use_global_device_ids=true | all-gather | bytes 10240 | tf_op jit(solution)/shard_map/all_gather | solution.py:78
  72.0 0.1 copy.23
  72.1 15.2 %all-gather.2.cloned.1.call-done = bf16[128,4096]{1,0:T(8,128)(2,1)} async-done(((bf16[128,1024]{1,0:T(8,128)(2,1)}), bf16[128,4096]{1,0:T(8,128)(2,1)}) %all-gather.2.cloned.1.call-update) | async-done | bytes 1048592 | tf_op jit(solution)/shard_map/all_gather | solution.py:77
  87.3 0.0 copy-start
  87.3 0.6 mul.46
  87.9 0.6 copy-done
  88.5 2.2 %fusion.14 = bf16[1,128,4096]{2,1,0:T(8,128)(2,1)} fusion(f32[16,8,32,128]{3,2,1,0:T(8,128)S(1)} %bitcast.69, bf16[128,4096]{1,0:T(8,128)(2,1)S(1)} %copy-done), kind=kLoop, calls=%fused_computation.21 | loop fusion | flops 1572864 | bytes 4194304 | tf_op jit(solution)/shard_map/broadcast_in_dim | solution.py:81
  (9 shorter events, 0.1 us)
Async XLA Ops:
  8.1 3.3 %copy-start.2 = (bf16[1,1,2,128,128]{4,3,2,1,0:T(8,128)(2,1)S(1)}, bf16[1,1,2,128,128]{4,3,2,1,0:T(8,128)(2,1)}, u32[]{:S(2)}) copy-start(bf16[1,1,2,128,128]{4,3,2,1,0:T(8,128)(2,1)} %param.7) | copy-start | bytes 196612
  11.4 1.5 %copy-start.1 = (bf16[1,1,2,3584,128]{4,3,2,1,0:T(8,128)(2,1)S(1)}, bf16[1,1,2,3584,128]{4,3,2,1,0:T(8,128)(2,1)}, u32[]{:S(2)}) copy-start(bf16[1,1,2,3584,128]{4,3,2,1,0:T(8,128)(2,1)} %param.6) | copy-start | bytes 5505028
  30.8 28.1 %all-to-all-start = ((bf16[128,4,1024]{0,2,1:T(8,128)(2,1)}), bf16[128,4,1024]{0,2,1:T(8,128)(2,1)S(1)}, u32[]{:S(2)}, u32[]{:S(2)}) async-start(bf16[128,4,1024]{0,2,1:T(8,128)(2,1)} %bitcast.17), calls=%async_computation | async-start | bytes 2097152 | tf_op jit(solution)/shard_map/all_to_all | solution.py:73
  34.3 53.0 %all-gather.2.cloned.1.call-start = ((), (), s32[]{:S(2)}) async-start(), calls=%async_computation.2 | async-start | bytes 1310720 | tf_op jit(solution)/shard_map/all_gather | solution.py:77
  87.3 1.2 %copy-start = (bf16[128,4096]{1,0:T(8,128)(2,1)S(1)}, bf16[128,4096]{1,0:T(8,128)(2,1)}, u32[]{:S(2)}) copy-start(bf16[128,4096]{1,0:T(8,128)(2,1)} %all-gather.2.cloned.1.call-done) | copy-start | bytes 3145732
Sparse Core Ops, SparseCore 0:
  60.2 27.0 all-gather.1
where the time goes:
time: 98 us; the launch traced here: 97.6 us
  waiting for transfers between devices  39.7 us (41%)
  blocking collectives  23.6 us (24%)
  between operations  14.2 us (14%)
  local copies, waits for them, and re-layouts  7.11 us (7%)
  matrix products  5.09 us (5%)
  other arithmetic  4.34 us (4%)
  starting transfers between devices  3.56 us (4%)
    all_to_all x1, waiting for transfers between devices, per_device(): lax.all_to_all(outgoing[0], 'tp', split_axis=1, concat_axis=1, tiled=True)  24.5 us
    all_gather x1, waiting for transfers between devices, per_device(): lax.all_gather(recoded, 'tp', axis=1, tiled=True)  15.2 us
    all_gather x1, blocking collectives, per_device(): lax.all_gather(rescales, 'tp', axis=1, tiled=True)  11.9 us
    all_to_all x1, blocking collectives, per_device(): lax.all_to_all(outgoing[1], 'tp', split_axis=1, concat_axis=1, tiled=True)  11.7 us
    all_to_all x1, starting transfers between devices, per_device(): lax.all_to_all(outgoing[0], 'tp', split_axis=1, concat_axis=1, tiled=True)  3.52 us
    dot_general x1, matrix products, attend(): jnp.einsum('ckd,pd->kcp', query_heads, past_kv[0], preferred_element_type...  3.32 us
    dot_general x1, local copies, waits for them, and re-layouts, per_device(): jnp.dot(attended, out_weight, preferred_element_type=jnp.float32)  3.28 us
    broadcast_in_dim x1, other arithmetic, per_device(): return mixed[None]  2.19 us
  transfers between devices with their start and end apart: 2, of which 2 were waited for; matrix products, arithmetic and copies ran while one was open for 0% of the time, Pallas kernels for 0%

commit v1 on v0

v1 whole, which is shorter than its diff:
```python
import functools
import math

import jax
import jax.numpy as jnp
from jax import lax
from jax.experimental import pallas as pl
from jax.experimental.pallas import tpu as pltpu
from jax.sharding import PartitionSpec as P

HD = 128
HQ_DEV = 2
CH = 128
SAFE = 896
TILE = 512
CHUNK = 256
LAG = 4
MASKED = -1e30
MESH = pl.DeviceIdType.MESH
NT = (((1,), (1,)), ((), ()))


def kernel(n, q_ref, cache_ref, new_ref, w_hbm, prefix_ref, out_ref,
           kv, weight, scores, attended, stage, landed,
           load_sem, rs_send, rs_recv, ag_send, ag_recv):
    t = lax.axis_index("tp")
    pmax = cache_ref.shape[1]
    dw = w_hbm.shape[1]
    half = dw // 2
    count = half // CHUNK
    has_prev = t > 0
    has_next = t < n - 1
    prev, nxt = jnp.maximum(t - 1, 0), jnp.minimum(t + 1, n - 1)

    loads = [
        pltpu.make_async_copy(cache_ref.at[0], kv.at[0], load_sem.at[0]),
        pltpu.make_async_copy(cache_ref.at[1], kv.at[1], load_sem.at[1]),
        pltpu.make_async_copy(w_hbm, weight, load_sem.at[2]),
    ]
    for load in loads:
        load.start()

    barrier = pltpu.get_barrier_semaphore()

    @pl.when(has_prev)
    def _():
        pl.semaphore_signal(barrier, inc=1, device_id={"tp": prev}, device_id_type=MESH)

    @pl.when(has_next)
    def _():
        pl.semaphore_signal(barrier, inc=1, device_id={"tp": nxt}, device_id_type=MESH)

    factor = HD ** -0.5 * math.log2(math.e)
    length = prefix_ref[0]
    rows = HQ_DEV * CH
    query = jnp.concatenate([q_ref[:, h * HD:(h + 1) * HD] for h in range(HQ_DEV)], axis=0)
    top = jnp.full((rows, 128), MASKED, jnp.float32)

    def widest(top, tile):
        for j in range(tile.shape[1] // 128):
            top = jnp.maximum(top, tile[:, j * 128:(j + 1) * 128])
        return top

    row = lax.broadcasted_iota(jnp.int32, (rows, CH), 0) % CH
    col = lax.broadcasted_iota(jnp.int32, (rows, CH), 1)
    fresh = lax.dot_general(query, new_ref[0], NT, preferred_element_type=jnp.float32)
    fresh = jnp.where(col <= row, fresh, MASKED)
    top = widest(top, fresh)
    loads[0].wait()
    for start in range(0, pmax, TILE):
        size = min(TILE, pmax - start)
        tile = lax.dot_general(query, kv[0, start:start + size], NT, preferred_element_type=jnp.float32)
        if start + size > SAFE:
            slot = lax.broadcasted_iota(jnp.int32, (1, size), 1) + start
            tile = jnp.where(slot < length, tile, MASKED)
        scores[:, start:start + size] = tile
        top = widest(top, tile)
    highest = jnp.max(top, axis=1, keepdims=True) * factor

    def weigh(tile, total):
        weights = jnp.exp2(tile * factor - highest)
        for j in range(tile.shape[1] // 128):
            total = total + weights[:, j * 128:(j + 1) * 128]
        return weights.astype(jnp.bfloat16), total

    total = jnp.zeros((rows, 128), jnp.float32)
    weights, total = weigh(fresh, total)
    summed = jnp.dot(weights, new_ref[1], preferred_element_type=jnp.float32)
    loads[1].wait()
    for start in range(0, pmax, TILE):
        size = min(TILE, pmax - start)
        weights, total = weigh(scores[:, start:start + size], total)
        summed = summed + jnp.dot(weights, kv[1, start:start + size], preferred_element_type=jnp.float32)
    summed = summed / jnp.sum(total, axis=1, keepdims=True)
    for h in range(HQ_DEV):
        attended[:, h * HD:(h + 1) * HD] = summed[h * CH:(h + 1) * CH].astype(jnp.bfloat16)

    loads[2].wait()
    pl.semaphore_wait(barrier, has_prev.astype(jnp.int32) + has_next.astype(jnp.int32))

    towards = (nxt, prev)
    back = (prev, nxt)
    is_first = (t == 0, t == n - 1)
    is_owner = (t == n - 1, t == 0)

    def columns(d, i):
        return pl.ds(pl.multiple_of((1 - d) * half + i * CHUNK, CHUNK), CHUNK)

    def sum_copy(d, i):
        return pltpu.make_async_remote_copy(
            src_ref=stage.at[d, i], dst_ref=landed.at[d, i],
            send_sem=rs_send.at[d, i], recv_sem=rs_recv.at[d, i],
            device_id={"tp": towards[d]}, device_id_type=MESH)

    def result_copy(d, i):
        return pltpu.make_async_remote_copy(
            src_ref=out_ref.at[:, columns(d, i)], dst_ref=out_ref.at[:, columns(d, i)],
            send_sem=ag_send.at[d, i], recv_sem=ag_recv.at[d, i],
            device_id={"tp": back[d]}, device_id_type=MESH)

    def sum_step(d, i):
        part = jnp.dot(attended[...], weight[:, columns(d, i)], preferred_element_type=jnp.float32)

        @pl.when(is_first[d])
        def _():
            stage[d, i] = part.astype(jnp.bfloat16)
            sum_copy(d, i).start()

        @pl.when(jnp.logical_not(is_first[d]))
        def _():
            sum_copy(d, i).wait_recv()
            running = (part + landed[d, i].astype(jnp.float32)).astype(jnp.bfloat16)

            @pl.when(is_owner[d])
            def _():
                out_ref[:, columns(d, i)] = running
                result_copy(d, i).start()

            @pl.when(jnp.logical_not(is_owner[d]))
            def _():
                stage[d, i] = running
                sum_copy(d, i).start()

    def result_step(d, i):
        @pl.when(jnp.logical_not(is_owner[d]))
        def _():
            result_copy(d, i).wait_recv()

            @pl.when(jnp.logical_not(is_first[d]))
            def _():
                result_copy(d, i).start()

    lag = min(LAG, count)

    @pl.loop(0, lag)
    def _(i):
        for d in range(2):
            sum_step(d, i)

    @pl.loop(lag, count)
    def _(i):
        for d in range(2):
            sum_step(d, i)
        for d in range(2):
            result_step(d, i - lag)

    @pl.loop(count - lag, count)
    def _(i):
        for d in range(2):
            result_step(d, i)

    @pl.loop(0, count)
    def _(i):
        for d in range(2):
            @pl.when(jnp.logical_not(is_owner[d]))
            def _():
                sum_copy(d, i).wait_send()

            @pl.when(jnp.logical_not(is_first[d]))
            def _():
                result_copy(d, i).wait_send()


def per_device(queries, cache, new_kv, out_weight, prefix):
    n = lax.axis_size("tp")
    pmax = cache.shape[3]
    dw = out_weight.shape[1]
    count = dw // 2 // CHUNK
    vmem = pl.BlockSpec(memory_space=pltpu.VMEM)
    hbm = pl.BlockSpec(memory_space=pl.ANY)
    out = pl.pallas_call(
        functools.partial(kernel, n),
        out_shape=jax.ShapeDtypeStruct((CH, dw), jnp.bfloat16),
        in_specs=[vmem, hbm, vmem, hbm, pl.BlockSpec(memory_space=pltpu.SMEM)],
        out_specs=vmem,
        scratch_shapes=[
            pltpu.VMEM((2, pmax, HD), jnp.bfloat16),
            pltpu.VMEM(out_weight.shape, jnp.bfloat16),
            pltpu.VMEM((HQ_DEV * CH, pmax), jnp.float32),
            pltpu.VMEM((CH, HQ_DEV * HD), jnp.bfloat16),
            pltpu.VMEM((2, count, CH, CHUNK), jnp.bfloat16),
            pltpu.VMEM((2, count, CH, CHUNK), jnp.bfloat16),
            pltpu.SemaphoreType.DMA((3,)),
            pltpu.SemaphoreType.DMA((2, count)),
            pltpu.SemaphoreType.DMA((2, count)),
            pltpu.SemaphoreType.DMA((2, count)),
            pltpu.SemaphoreType.DMA((2, count)),
        ],
        compiler_params=pltpu.CompilerParams(
            collective_id=0, has_side_effects=True, vmem_limit_bytes=48 * 1024 * 1024),
    )(queries[0], cache[0, 0], new_kv[0, 0], out_weight, prefix)
    return out[None]


def solution(mesh):
    in_specs = (
        P(("groups", "dp"), None, "tp"),
        P(("groups", "dp"), "tp", None, None, None),
        P(("groups", "dp"), "tp", None, None, None),
        P("tp", None),
        P(("groups", "dp")),
    )
    out_specs = P(("groups", "dp"), None, None)
    return jax.shard_map(
        per_device, mesh=mesh, in_specs=in_specs, out_specs=out_specs, check_vma=False
    )
```

time: 98 us -> 209 us (2.13)
  Pallas kernels: 0 us -> 203 us
  waiting for transfers between devices: 39.7 us -> 0 us
  blocking collectives: 23.6 us -> 0 us
  between operations: 14.2 us -> 0.67 us
  matrix products: 5.09 us -> 0 us
  other arithmetic: 4.34 us -> 0 us
  starting transfers between devices: 3.56 us -> 0 us
    pallas_call x0 -> x1, Pallas kernels: none -> 203 us  [per_device(): pl.pallas_call(functools.partial(kernel, n), out_shape=jax.ShapeDtypeStru...]
    all_to_all x1 -> x0, waiting for transfers between devices: 24.5 us -> none  [per_device(): lax.all_to_all(outgoing[0], 'tp', split_axis=1, concat_axis=1, tiled=True)]
    all_gather x1 -> x0, waiting for transfers between devices: 15.2 us -> none  [per_device(): lax.all_gather(recoded, 'tp', axis=1, tiled=True)]
    all_gather x1 -> x0, blocking collectives: 11.9 us -> none  [per_device(): lax.all_gather(rescales, 'tp', axis=1, tiled=True)]
    all_to_all x1 -> x0, blocking collectives: 11.7 us -> none  [per_device(): lax.all_to_all(outgoing[1], 'tp', split_axis=1, concat_axis=1, tiled=True)]
    dot_general x5 -> x0, matrix products: 5.09 us -> none  [the longest x1 3.32 us: attend(): jnp.einsum('ckd,pd->kcp', query_heads, past_kv[0], preferred_element_type...]
    unnamed x6 -> x9, local copies, waits for them, and re-layouts: 1.42 us -> 5.73 us
    all_to_all x1 -> x0, starting transfers between devices: 3.52 us -> none  [per_device(): lax.all_to_all(outgoing[0], 'tp', split_axis=1, concat_axis=1, tiled=True)]
  transfers between devices with their start and end apart: 2 -> 0, of which waited for: 2 -> 0; matrix products, arithmetic and copies ran while one was open for 0% -> 0% of each run, Pallas kernels for 0% -> 0%
where the time goes in v1:
time: 209 us
  Pallas kernels  203 us (97%)
  local copies, waits for them, and re-layouts  5.73 us (3%)
    pallas_call x1, Pallas kernels, per_device(): pl.pallas_call(functools.partial(kernel, n), out_shape=jax.ShapeDtypeStru...  203 us
    unnamed x9, local copies, waits for them, and re-layouts  5.73 us

profile of v1, /device:TPU:0, one launch (start us, length us, event | category | flops | bytes accessed | tf_op | source)
XLA Modules:
  0.0 209.0 jit_solution(1419414629035382187)
XLA Ops:
  0.7 0.0 copy-start
  0.7 1.6 copy-done
  2.2 0.0 copy-start.1
  2.2 1.5 copy-done.1
  3.7 0.0 copy-start.2
  3.7 0.8 copy-done.2
  4.6 0.0 copy-start.3
  4.6 0.8 copy-done.3
  5.4 202.5 %shard_map.55 = bf16[128,4096]{1,0:T(8,128)(2,1)S(1)} custom-call(bf16[128,256]{1,0:T(8,128)(2,1)S(1)} %bitcast.6, bf16[2,3584,128]{2,1,0:T(8,128)(2,1)S(1)} %bitcast.5, bf16[2,128,128]{2,1,0:T(8,128)(2,1)S(1)} %bitcast.7, bf16[256,4096]{1,0:T(8,128)(2,1)S(1)} %copy-done, s32[1]{0:T(128)S(6)} %copy.7.prefix_ref), custom_call_target="tpu_custom_call" | custom-call | tf_op jit(solution)/shard_map/pallas_call | solution.py:191
  208.0 1.0 copy.8
Async XLA Ops:
  0.7 1.6 copy-start
  2.2 1.5 copy-start.1
  3.7 0.8 copy-start.2
  4.6 0.8 copy-start.3

commit v2 on v1

--- a/solution.py
+++ b/solution.py
@@ -14,15 +14,15 @@
 SAFE = 896
 TILE = 512
 CHUNK = 256
-LAG = 4
+SKEW = 2
 MASKED = -1e30
 MESH = pl.DeviceIdType.MESH
 NT = (((1,), (1,)), ((), ()))
 
 
 def kernel(n, q_ref, cache_ref, new_ref, w_hbm, prefix_ref, out_ref,
-           kv, weight, scores, attended, stage, landed,
-           load_sem, rs_send, rs_recv, ag_send, ag_recv):
+           query2, fresh_kv, kv, weight, scores, attended, stage, landed,
+           results, load_sem, rs_send, rs_recv, ag_send, ag_recv):
     t = lax.axis_index("tp")
     pmax = cache_ref.shape[1]
     dw = w_hbm.shape[1]
@@ -33,6 +33,8 @@
     prev, nxt = jnp.maximum(t - 1, 0), jnp.minimum(t + 1, n - 1)
 
     loads = [
+        pltpu.make_async_copy(q_ref, query2, load_sem.at[3]),
+        pltpu.make_async_copy(new_ref, fresh_kv, load_sem.at[4]),
         pltpu.make_async_copy(cache_ref.at[0], kv.at[0], load_sem.at[0]),
         pltpu.make_async_copy(cache_ref.at[1], kv.at[1], load_sem.at[1]),
         pltpu.make_async_copy(w_hbm, weight, load_sem.at[2]),
@@ -53,7 +55,9 @@
     factor = HD ** -0.5 * math.log2(math.e)
     length = prefix_ref[0]
     rows = HQ_DEV * CH
-    query = jnp.concatenate([q_ref[:, h * HD:(h + 1) * HD] for h in range(HQ_DEV)], axis=0)
+    loads[0].wait()
+    loads[1].wait()
+    query = jnp.concatenate([query2[:, h * HD:(h + 1) * HD] for h in range(HQ_DEV)], axis=0)
     top = jnp.full((rows, 128), MASKED, jnp.float32)
 
     def widest(top, tile):
@@ -63,10 +67,10 @@
 
     row = lax.broadcasted_iota(jnp.int32, (rows, CH), 0) % CH
     col = lax.broadcasted_iota(jnp.int32, (rows, CH), 1)
-    fresh = lax.dot_general(query, new_ref[0], NT, preferred_element_type=jnp.float32)
+    fresh = lax.dot_general(query, fresh_kv[0], NT, preferred_element_type=jnp.float32)
     fresh = jnp.where(col <= row, fresh, MASKED)
     top = widest(top, fresh)
-    loads[0].wait()
+    loads[2].wait()
     for start in range(0, pmax, TILE):
         size = min(TILE, pmax - start)
         tile = lax.dot_general(query, kv[0, start:start + size], NT, preferred_element_type=jnp.float32)
@@ -85,8 +89,8 @@
 
     total = jnp.zeros((rows, 128), jnp.float32)
     weights, total = weigh(fresh, total)
-    summed = jnp.dot(weights, new_ref[1], preferred_element_type=jnp.float32)
-    loads[1].wait()
+    summed = jnp.dot(weights, fresh_kv[1], preferred_element_type=jnp.float32)
+    loads[3].wait()
     for start in range(0, pmax, TILE):
         size = min(TILE, pmax - start)
         weights, total = weigh(scores[:, start:start + size], total)
@@ -95,7 +99,7 @@
     for h in range(HQ_DEV):
         attended[:, h * HD:(h + 1) * HD] = summed[h * CH:(h + 1) * CH].astype(jnp.bfloat16)
 
-    loads[2].wait()
+    loads[4].wait()
     pl.semaphore_wait(barrier, has_prev.astype(jnp.int32) + has_next.astype(jnp.int32))
 
     towards = (nxt, prev)
@@ -114,7 +118,7 @@
 
     def result_copy(d, i):
         return pltpu.make_async_remote_copy(
-            src_ref=out_ref.at[:, columns(d, i)], dst_ref=out_ref.at[:, columns(d, i)],
+            src_ref=results.at[d, i], dst_ref=results.at[d, i],
             send_sem=ag_send.at[d, i], recv_sem=ag_recv.at[d, i],
             device_id={"tp": back[d]}, device_id_type=MESH)
 
@@ -133,6 +137,7 @@
 
             @pl.when(is_owner[d])
             def _():
+                results[d, i] = running
                 out_ref[:, columns(d, i)] = running
                 result_copy(d, i).start()
 
@@ -150,24 +155,20 @@
             def _():
                 result_copy(d, i).start()
 
-    lag = min(LAG, count)
-
-    @pl.loop(0, lag)
-    def _(i):
-        for d in range(2):
-            sum_step(d, i)
-
-    @pl.loop(lag, count)
-    def _(i):
-        for d in range(2):
-            sum_step(d, i)
-        for d in range(2):
-            result_step(d, i - lag)
-
-    @pl.loop(count - lag, count)
-    def _(i):
-        for d in range(2):
-            result_step(d, i)
+            out_ref[:, columns(d, i)] = results[d, i]
+
+    far = n - 1
+    hops = ((t, far - t), (far + far - t, far + t))
+
+    @pl.loop(0, count + 2 * far * SKEW)
+    def _(step):
+        for delays, work in zip(hops, (sum_step, result_step)):
+            for d in range(2):
+                i = step - delays[d] * SKEW
+
+                @pl.when((i >= 0) & (i < count))
+                def _():
+                    work(d, i)
 
     @pl.loop(0, count)
     def _(i):
@@ -187,20 +188,23 @@
     dw = out_weight.shape[1]
     count = dw // 2 // CHUNK
     vmem = pl.BlockSpec(memory_space=pltpu.VMEM)
-    hbm = pl.BlockSpec(memory_space=pl.ANY)
+    hbm = pl.BlockSpec(memory_space=pltpu.HBM)
     out = pl.pallas_call(
         functools.partial(kernel, n),
         out_shape=jax.ShapeDtypeStruct((CH, dw), jnp.bfloat16),
-        in_specs=[vmem, hbm, vmem, hbm, pl.BlockSpec(memory_space=pltpu.SMEM)],
+        in_specs=[hbm, hbm, hbm, hbm, pl.BlockSpec(memory_space=pltpu.SMEM)],
         out_specs=vmem,
         scratch_shapes=[
+            pltpu.VMEM((CH, HQ_DEV * HD), jnp.bfloat16),
+            pltpu.VMEM((2, CH, HD), jnp.bfloat16),
             pltpu.VMEM((2, pmax, HD), jnp.bfloat16),
             pltpu.VMEM(out_weight.shape, jnp.bfloat16),
             pltpu.VMEM((HQ_DEV * CH, pmax), jnp.float32),
             pltpu.VMEM((CH, HQ_DEV * HD), jnp.bfloat16),
             pltpu.VMEM((2, count, CH, CHUNK), jnp.bfloat16),
             pltpu.VMEM((2, count, CH, CHUNK), jnp.bfloat16),
-            pltpu.SemaphoreType.DMA((3,)),
+            pltpu.VMEM((2, count, CH, CHUNK), jnp.bfloat16),
+            pltpu.SemaphoreType.DMA((5,)),
             pltpu.SemaphoreType.DMA((2, count)),
             pltpu.SemaphoreType.DMA((2, count)),
             pltpu.SemaphoreType.DMA((2, count)),

time: 209 us -> 47.7 us (0.23)
  Pallas kernels: 203 us -> 41 us
    pallas_call x1, Pallas kernels: 203 us -> 41 us  [per_device(): pl.pallas_call(functools.partial(kernel, n), out_shape=jax.ShapeDtypeStru...]
where the time goes in v2:
time: 47.7 us; the launch traced here: 47.4 us
  Pallas kernels  41 us (86%)
  local copies, waits for them, and re-layouts  5.73 us (12%)
  between operations  0.67 us (1%)
    pallas_call x1, Pallas kernels, per_device(): pl.pallas_call(functools.partial(kernel, n), out_shape=jax.ShapeDtypeStru...  41 us
    unnamed x9, local copies, waits for them, and re-layouts  5.73 us

profile of v2, /device:TPU:0, one launch (start us, length us, event | category | flops | bytes accessed | tf_op | source)
XLA Modules:
  0.0 47.4 jit_solution(5606030163938905111)
XLA Ops:
  0.7 0.0 copy-start
  0.7 1.6 %copy-done = bf16[256,4096]{1,0:T(8,128)(2,1)S(1)} copy-done((bf16[256,4096]{1,0:T(8,128)(2,1)S(1)}, bf16[256,4096]{1,0:T(8,128)(2,1)}, u32[]{:S(2)}) %copy-start) | copy-done | bytes 2097176
  2.2 0.0 copy-start.1
  2.2 1.5 %copy-done.1 = bf16[1,1,2,3584,128]{4,3,2,1,0:T(8,128)(2,1)S(1)} copy-done((bf16[1,1,2,3584,128]{4,3,2,1,0:T(8,128)(2,1)S(1)}, bf16[1,1,2,3584,128]{4,3,2,1,0:T(8,128)(2,1)}, u32[]{:S(2)}) %copy-start.1) | copy-done | bytes 1835032
  3.7 0.0 copy-start.2
  3.7 0.8 %copy-done.2 = bf16[1,128,256]{2,1,0:T(8,128)(2,1)S(1)} copy-done((bf16[1,128,256]{2,1,0:T(8,128)(2,1)S(1)}, bf16[1,128,256]{2,1,0:T(8,128)(2,1)}, u32[]{:S(2)}) %copy-start.2) | copy-done | bytes 65560
  4.6 0.0 copy-start.3
  4.6 0.8 %copy-done.3 = bf16[1,1,2,128,128]{4,3,2,1,0:T(8,128)(2,1)S(1)} copy-done((bf16[1,1,2,128,128]{4,3,2,1,0:T(8,128)(2,1)S(1)}, bf16[1,1,2,128,128]{4,3,2,1,0:T(8,128)(2,1)}, u32[]{:S(2)}) %copy-start.3) | copy-done | bytes 65560
  5.4 41.0 %shard_map.55 = bf16[128,4096]{1,0:T(8,128)(2,1)S(1)} custom-call(bf16[128,256]{1,0:T(8,128)(2,1)S(1)} %bitcast.6, bf16[2,3584,128]{2,1,0:T(8,128)(2,1)S(1)} %bitcast.5, bf16[2,128,128]{2,1,0:T(8,128)(2,1)S(1)} %bitcast.7, bf16[256,4096]{1,0:T(8,128)(2,1)S(1)} %copy-done, s32[1]{0:T(128)S(6)} %copy.7.prefix_ref), custom_call_target="tpu_custom_call" | custom-call | tf_op jit(solution)/shard_map/pallas_call | solution.py:192
  46.4 1.0 %copy.8 = bf16[1,128,4096]{2,1,0:T(8,128)(2,1)} copy(bf16[1,128,4096]{2,1,0:T(8,128)(2,1)S(1)} %bitcast.4) | data formatting | bytes 2097152
Async XLA Ops:
  0.7 1.6 %copy-start = (bf16[256,4096]{1,0:T(8,128)(2,1)S(1)}, bf16[256,4096]{1,0:T(8,128)(2,1)}, u32[]{:S(2)}) copy-start(bf16[256,4096]{1,0:T(8,128)(2,1)} %w_hbm.1) | copy-start | bytes 6291460
  2.2 1.5 %copy-start.1 = (bf16[1,1,2,3584,128]{4,3,2,1,0:T(8,128)(2,1)S(1)}, bf16[1,1,2,3584,128]{4,3,2,1,0:T(8,128)(2,1)}, u32[]{:S(2)}) copy-start(bf16[1,1,2,3584,128]{4,3,2,1,0:T(8,128)(2,1)} %param.6) | copy-start | bytes 5505028
  3.7 0.8 %copy-start.2 = (bf16[1,128,256]{2,1,0:T(8,128)(2,1)S(1)}, bf16[1,128,256]{2,1,0:T(8,128)(2,1)}, u32[]{:S(2)}) copy-start(bf16[1,128,256]{2,1,0:T(8,128)(2,1)} %param.5) | copy-start | bytes 196612
  4.6 0.8 %copy-start.3 = (bf16[1,1,2,128,128]{4,3,2,1,0:T(8,128)(2,1)S(1)}, bf16[1,1,2,128,128]{4,3,2,1,0:T(8,128)(2,1)}, u32[]{:S(2)}) copy-start(bf16[1,1,2,128,128]{4,3,2,1,0:T(8,128)(2,1)} %param.7) | copy-start | bytes 196612

commit v3 on v2

--- a/solution.py
+++ b/solution.py
@@ -13,15 +13,15 @@
 CH = 128
 SAFE = 896
 TILE = 512
-CHUNK = 256
-SKEW = 2
+CHUNK = 128
+SKEW = 5
 MASKED = -1e30
 MESH = pl.DeviceIdType.MESH
 NT = (((1,), (1,)), ((), ()))
 
 
 def kernel(n, q_ref, cache_ref, new_ref, w_hbm, prefix_ref, out_ref,
-           query2, fresh_kv, kv, weight, scores, attended, stage, landed,
+           query2, fresh_kv, kv, weight, scores, attended, parts, stage, landed,
            results, load_sem, rs_send, rs_recv, ag_send, ag_recv):
     t = lax.axis_index("tp")
     pmax = cache_ref.shape[1]
@@ -122,8 +122,11 @@
             send_sem=ag_send.at[d, i], recv_sem=ag_recv.at[d, i],
             device_id={"tp": back[d]}, device_id_type=MESH)
 
+    def project(d, i):
+        parts[d, i] = jnp.dot(attended[...], weight[:, columns(d, i)], preferred_element_type=jnp.float32)
+
     def sum_step(d, i):
-        part = jnp.dot(attended[...], weight[:, columns(d, i)], preferred_element_type=jnp.float32)
+        part = parts[d, i]
 
         @pl.when(is_first[d])
         def _():
@@ -139,7 +142,6 @@
             def _():
                 results[d, i] = running
                 out_ref[:, columns(d, i)] = running
-                result_copy(d, i).start()
 
             @pl.when(jnp.logical_not(is_owner[d]))
             def _():
@@ -147,6 +149,10 @@
                 sum_copy(d, i).start()
 
     def result_step(d, i):
+        @pl.when(is_owner[d])
+        def _():
+            result_copy(d, i).start()
+
         @pl.when(jnp.logical_not(is_owner[d]))
         def _():
             result_copy(d, i).wait_recv()
@@ -158,13 +164,18 @@
             out_ref[:, columns(d, i)] = results[d, i]
 
     far = n - 1
-    hops = ((t, far - t), (far + far - t, far + t))
-
-    @pl.loop(0, count + 2 * far * SKEW)
+    turn = max(count, far * SKEW)
+    hops = (t * SKEW, (far - t) * SKEW)
+
+    @pl.loop(-1, turn + count + far * SKEW)
     def _(step):
-        for delays, work in zip(hops, (sum_step, result_step)):
+        for work, delays in (
+            (sum_step, hops),
+            (result_step, (turn + hops[1], turn + hops[0])),
+            (project, (hops[0] - 1, hops[1] - 1)),
+        ):
             for d in range(2):
-                i = step - delays[d] * SKEW
+                i = step - delays[d]
 
                 @pl.when((i >= 0) & (i < count))
                 def _():
@@ -201,6 +212,7 @@
             pltpu.VMEM(out_weight.shape, jnp.bfloat16),
             pltpu.VMEM((HQ_DEV * CH, pmax), jnp.float32),
             pltpu.VMEM((CH, HQ_DEV * HD), jnp.bfloat16),
+            pltpu.VMEM((2, count, CH, CHUNK), jnp.float32),
             pltpu.VMEM((2, count, CH, CHUNK), jnp.bfloat16),
             pltpu.VMEM((2, count, CH, CHUNK), jnp.bfloat16),
             pltpu.VMEM((2, count, CH, CHUNK), jnp.bfloat16),
@@ -211,7 +223,7 @@
             pltpu.SemaphoreType.DMA((2, count)),
         ],
         compiler_params=pltpu.CompilerParams(
-            collective_id=0, has_side_effects=True, vmem_limit_bytes=48 * 1024 * 1024),
+            collective_id=0, has_side_effects=True, vmem_limit_bytes=63 * 1024 * 1024),
     )(queries[0], cache[0, 0], new_kv[0, 0], out_weight, prefix)
     return out[None]
 

time: 47.7 us -> 41.6 us (0.87)
  local copies, waits for them, and re-layouts: 5.73 us -> 2.29 us
  Pallas kernels: 41 us -> 38.5 us
    unnamed x9 -> x1, local copies, waits for them, and re-layouts: 5.73 us -> 2.29 us
    pallas_call x1, Pallas kernels: 41 us -> 38.5 us  [per_device(): pl.pallas_call(functools.partial(kernel, n), out_shape=jax.ShapeDtypeStru...]
where the time goes in v3:
time: 41.6 us; the launch traced here: 41.5 us
  Pallas kernels  38.5 us (93%)
  local copies, waits for them, and re-layouts  2.29 us (6%)
  between operations  0.66 us (2%)
    pallas_call x1, Pallas kernels, per_device(): pl.pallas_call(functools.partial(kernel, n), out_shape=jax.ShapeDtypeStru...  38.5 us
    unnamed x1, local copies, waits for them, and re-layouts  2.29 us

profile of v3, /device:TPU:0, one launch (start us, length us, event | category | flops | bytes accessed | tf_op | source)
XLA Modules:
  0.0 41.5 jit_solution(131535602758286965)
XLA Ops:
  0.7 38.5 %shard_map.55 = bf16[128,4096]{1,0:T(8,128)(2,1)} custom-call(bf16[128,256]{1,0:T(8,128)(2,1)} %bitcast.6, bf16[2,3584,128]{2,1,0:T(8,128)(2,1)} %bitcast.5, bf16[2,128,128]{2,1,0:T(8,128)(2,1)} %bitcast.7, bf16[256,4096]{1,0:T(8,128)(2,1)} %w_hbm.1, s32[1]{0:T(128)S(6)} %copy.7.prefix_ref), custom_call_target="tpu_custom_call" | custom-call | tf_op jit(solution)/shard_map/pallas_call | solution.py:203
  39.2 2.3 %copy.8 = bf16[1,128,4096]{2,1,0:T(8,128)(2,1)} copy(bf16[1,128,4096]{2,1,0:T(8,128)(2,1)} %bitcast.4) | data formatting | bytes 2097152

commit v4 on v3

--- a/solution.py
+++ b/solution.py
@@ -13,7 +13,8 @@
 CH = 128
 SAFE = 896
 TILE = 512
-CHUNK = 128
+WIDE = 256
+PARTS = 2
 SKEW = 5
 MASKED = -1e30
 MESH = pl.DeviceIdType.MESH
@@ -27,7 +28,9 @@
     pmax = cache_ref.shape[1]
     dw = w_hbm.shape[1]
     half = dw // 2
-    count = half // CHUNK
+    per_part = half // WIDE
+    count = PARTS * per_part
+    deep = CH // PARTS
     has_prev = t > 0
     has_next = t < n - 1
     prev, nxt = jnp.maximum(t - 1, 0), jnp.minimum(t + 1, n - 1)
@@ -54,61 +57,66 @@
 
     factor = HD ** -0.5 * math.log2(math.e)
     length = prefix_ref[0]
-    rows = HQ_DEV * CH
-    loads[0].wait()
-    loads[1].wait()
-    query = jnp.concatenate([query2[:, h * HD:(h + 1) * HD] for h in range(HQ_DEV)], axis=0)
-    top = jnp.full((rows, 128), MASKED, jnp.float32)
+    rows = HQ_DEV * deep
 
     def widest(top, tile):
         for j in range(tile.shape[1] // 128):
             top = jnp.maximum(top, tile[:, j * 128:(j + 1) * 128])
         return top
 
-    row = lax.broadcasted_iota(jnp.int32, (rows, CH), 0) % CH
-    col = lax.broadcasted_iota(jnp.int32, (rows, CH), 1)
-    fresh = lax.dot_general(query, fresh_kv[0], NT, preferred_element_type=jnp.float32)
-    fresh = jnp.where(col <= row, fresh, MASKED)
-    top = widest(top, fresh)
-    loads[2].wait()
-    for start in range(0, pmax, TILE):
-        size = min(TILE, pmax - start)
-        tile = lax.dot_general(query, kv[0, start:start + size], NT, preferred_element_type=jnp.float32)
-        if start + size > SAFE:
-            slot = lax.broadcasted_iota(jnp.int32, (1, size), 1) + start
-            tile = jnp.where(slot < length, tile, MASKED)
-        scores[:, start:start + size] = tile
-        top = widest(top, tile)
-    highest = jnp.max(top, axis=1, keepdims=True) * factor
-
-    def weigh(tile, total):
-        weights = jnp.exp2(tile * factor - highest)
-        for j in range(tile.shape[1] // 128):
-            total = total + weights[:, j * 128:(j + 1) * 128]
-        return weights.astype(jnp.bfloat16), total
-
-    total = jnp.zeros((rows, 128), jnp.float32)
-    weights, total = weigh(fresh, total)
-    summed = jnp.dot(weights, fresh_kv[1], preferred_element_type=jnp.float32)
-    loads[3].wait()
-    for start in range(0, pmax, TILE):
-        size = min(TILE, pmax - start)
-        weights, total = weigh(scores[:, start:start + size], total)
-        summed = summed + jnp.dot(weights, kv[1, start:start + size], preferred_element_type=jnp.float32)
-    summed = summed / jnp.sum(total, axis=1, keepdims=True)
-    for h in range(HQ_DEV):
-        attended[:, h * HD:(h + 1) * HD] = summed[h * CH:(h + 1) * CH].astype(jnp.bfloat16)
-
-    loads[4].wait()
-    pl.semaphore_wait(barrier, has_prev.astype(jnp.int32) + has_next.astype(jnp.int32))
+    def attend(part):
+        mine = slice(part * deep, (part + 1) * deep)
+        query = jnp.concatenate([query2[mine, h * HD:(h + 1) * HD] for h in range(HQ_DEV)], axis=0)
+        top = jnp.full((rows, 128), MASKED, jnp.float32)
+        row = lax.broadcasted_iota(jnp.int32, (rows, CH), 0) % deep + part * deep
+        col = lax.broadcasted_iota(jnp.int32, (rows, CH), 1)
+        fresh = lax.dot_general(query, fresh_kv[0], NT, preferred_element_type=jnp.float32)
+        fresh = jnp.where(col <= row, fresh, MASKED)
+        top = widest(top, fresh)
+        if part == 0:
+            loads[2].wait()
+        for start in range(0, pmax, TILE):
+            size = min(TILE, pmax - start)
+            tile = lax.dot_general(query, kv[0, start:start + size], NT, preferred_element_type=jnp.float32)
+            if start + size > SAFE:
+                slot = lax.broadcasted_iota(jnp.int32, (1, size), 1) + start
+                tile = jnp.where(slot < length, tile, MASKED)
+            scores[:, start:start + size] = tile
+            top = widest(top, tile)
+        highest = jnp.max(top, axis=1, keepdims=True) * factor
+
+        def weigh(tile, total):
+            weights = jnp.exp2(tile * factor - highest)
+            for j in range(tile.shape[1] // 128):
+                total = total + weights[:, j * 128:(j + 1) * 128]
+            return weights.astype(jnp.bfloat16), total
+
+        total = jnp.zeros((rows, 128), jnp.float32)
+        weights, total = weigh(fresh, total)
+        summed = jnp.dot(weights, fresh_kv[1], preferred_element_type=jnp.float32)
+        if part == 0:
+            loads[3].wait()
+        for start in range(0, pmax, TILE):
+            size = min(TILE, pmax - start)
+            weights, total = weigh(scores[:, start:start + size], total)
+            summed = summed + jnp.dot(weights, kv[1, start:start + size], preferred_element_type=jnp.float32)
+        summed = summed / jnp.sum(total, axis=1, keepdims=True)
+        for h in range(HQ_DEV):
+            attended[mine, h * HD:(h + 1) * HD] = summed[h * deep:(h + 1) * deep].astype(jnp.bfloat16)
+
+    loads[0].wait()
+    loads[1].wait()
 
     towards = (nxt, prev)
     back = (prev, nxt)
     is_first = (t == 0, t == n - 1)
     is_owner = (t == n - 1, t == 0)
 
+    def tokens(i):
+        return pl.ds(pl.multiple_of(i // per_part * deep, deep), deep)
+
     def columns(d, i):
-        return pl.ds(pl.multiple_of((1 - d) * half + i * CHUNK, CHUNK), CHUNK)
+        return pl.ds(pl.multiple_of((1 - d) * half + i % per_part * WIDE, WIDE), WIDE)
 
     def sum_copy(d, i):
         return pltpu.make_async_remote_copy(
@@ -122,13 +130,20 @@
             send_sem=ag_send.at[d, i], recv_sem=ag_recv.at[d, i],
             device_id={"tp": back[d]}, device_id_type=MESH)
 
+    early = count - per_part
+
     def project(d, i):
-        parts[d, i] = jnp.dot(attended[...], weight[:, columns(d, i)], preferred_element_type=jnp.float32)
+        @pl.when(jnp.logical_not(is_first[d]) | (i >= early))
+        def _():
+            parts[d, i] = product(d, i)
+
+    def product(d, i):
+        return jnp.dot(attended[tokens(i), :], weight[:, columns(d, i)], preferred_element_type=jnp.float32)
 
     def sum_step(d, i):
         part = parts[d, i]
 
-        @pl.when(is_first[d])
+        @pl.when(is_first[d] & (i >= early))
         def _():
             stage[d, i] = part.astype(jnp.bfloat16)
             sum_copy(d, i).start()
@@ -141,7 +156,7 @@
             @pl.when(is_owner[d])
             def _():
                 results[d, i] = running
-                out_ref[:, columns(d, i)] = running
+                out_ref[tokens(i), columns(d, i)] = running
 
             @pl.when(jnp.logical_not(is_owner[d]))
             def _():
@@ -161,7 +176,21 @@
             def _():
                 result_copy(d, i).start()
 
-            out_ref[:, columns(d, i)] = results[d, i]
+            out_ref[tokens(i), columns(d, i)] = results[d, i]
+
+    for part in range(PARTS):
+        attend(part)
+        if part == 0:
+            loads[4].wait()
+            pl.semaphore_wait(barrier, has_prev.astype(jnp.int32) + has_next.astype(jnp.int32))
+        if part < PARTS - 1:
+            for d in range(2):
+                @pl.when(is_first[d])
+                def _():
+                    @pl.loop(part * per_part, (part + 1) * per_part)
+                    def _(i):
+                        stage[d, i] = product(d, i).astype(jnp.bfloat16)
+                        sum_copy(d, i).start()
 
     far = n - 1
     turn = max(count, far * SKEW)
@@ -197,12 +226,13 @@
     n = lax.axis_size("tp")
     pmax = cache.shape[3]
     dw = out_weight.shape[1]
-    count = dw // 2 // CHUNK
+    count = PARTS * (dw // 2 // WIDE)
+    deep = CH // PARTS
     vmem = pl.BlockSpec(memory_space=pltpu.VMEM)
     hbm = pl.BlockSpec(memory_space=pltpu.HBM)
     out = pl.pallas_call(
         functools.partial(kernel, n),
-        out_shape=jax.ShapeDtypeStruct((CH, dw), jnp.bfloat16),
+        out_shape=pltpu.VMEM((CH, dw), jnp.bfloat16),
         in_specs=[hbm, hbm, hbm, hbm, pl.BlockSpec(memory_space=pltpu.SMEM)],
         out_specs=vmem,
         scratch_shapes=[
@@ -210,12 +240,12 @@
             pltpu.VMEM((2, CH, HD), jnp.bfloat16),
             pltpu.VMEM((2, pmax, HD), jnp.bfloat16),
             pltpu.VMEM(out_weight.shape, jnp.bfloat16),
-            pltpu.VMEM((HQ_DEV * CH, pmax), jnp.float32),
+            pltpu.VMEM((HQ_DEV * deep, pmax), jnp.float32),
             pltpu.VMEM((CH, HQ_DEV * HD), jnp.bfloat16),
-            pltpu.VMEM((2, count, CH, CHUNK), jnp.float32),
-            pltpu.VMEM((2, count, CH, CHUNK), jnp.bfloat16),
-            pltpu.VMEM((2, count, CH, CHUNK), jnp.bfloat16),
-            pltpu.VMEM((2, count, CH, CHUNK), jnp.bfloat16),
+            pltpu.VMEM((2, count, deep, WIDE), jnp.float32),
+            pltpu.VMEM((2, count, deep, WIDE), jnp.bfloat16),
+            pltpu.VMEM((2, count, deep, WIDE), jnp.bfloat16),
+            pltpu.VMEM((2, count, deep, WIDE), jnp.bfloat16),
             pltpu.SemaphoreType.DMA((5,)),
             pltpu.SemaphoreType.DMA((2, count)),
             pltpu.SemaphoreType.DMA((2, count)),
@@ -223,7 +253,7 @@
             pltpu.SemaphoreType.DMA((2, count)),
         ],
         compiler_params=pltpu.CompilerParams(
-            collective_id=0, has_side_effects=True, vmem_limit_bytes=63 * 1024 * 1024),
+            collective_id=0, has_side_effects=True, vmem_limit_bytes=60 * 1024 * 1024),
     )(queries[0], cache[0, 0], new_kv[0, 0], out_weight, prefix)
     return out[None]
 

time: 41.6 us -> 38.6 us (0.928)
  Pallas kernels: 38.5 us -> 36.9 us
  local copies, waits for them, and re-layouts: 2.29 us -> 0.97 us
    pallas_call x1, Pallas kernels: 38.5 us -> 36.9 us  [per_device(): pl.pallas_call(functools.partial(kernel, n), out_shape=pltpu.VMEM((CH, dw...]
    unnamed x1, local copies, waits for them, and re-layouts: 2.29 us -> 0.97 us
where the time goes in v4:
time: 38.6 us; the launch traced here: 38.5 us
  Pallas kernels  36.9 us (96%)
  local copies, waits for them, and re-layouts  0.97 us (3%)
  between operations  0.66 us (2%)
    pallas_call x1, Pallas kernels, per_device(): pl.pallas_call(functools.partial(kernel, n), out_shape=pltpu.VMEM((CH, dw...  36.9 us
    unnamed x1, local copies, waits for them, and re-layouts  0.97 us

profile of v4, /device:TPU:0, one launch (start us, length us, event | category | flops | bytes accessed | tf_op | source)
XLA Modules:
  0.0 38.5 jit_solution(14181300919633742484)
XLA Ops:
  0.7 36.9 %shard_map.55 = bf16[128,4096]{1,0:T(8,128)(2,1)S(1)} custom-call(bf16[128,256]{1,0:T(8,128)(2,1)} %bitcast.6, bf16[2,3584,128]{2,1,0:T(8,128)(2,1)} %bitcast.5, bf16[2,128,128]{2,1,0:T(8,128)(2,1)} %bitcast.7, bf16[256,4096]{1,0:T(8,128)(2,1)} %w_hbm.1, s32[1]{0:T(128)S(6)} %copy.8.prefix_ref), custom_call_target="tpu_custom_call" | custom-call | tf_op jit(solution)/shard_map/pallas_call | solution.py:233
  37.5 1.0 %copy.7 = bf16[1,128,4096]{2,1,0:T(8,128)(2,1)} copy(bf16[1,128,4096]{2,1,0:T(8,128)(2,1)S(1)} %bitcast.4) | data formatting | bytes 2097152

commit v5 on v4

--- a/solution.py
+++ b/solution.py
@@ -16,6 +16,7 @@
 WIDE = 256
 PARTS = 2
 SKEW = 5
+BEHIND = 4
 MASKED = -1e30
 MESH = pl.DeviceIdType.MESH
 NT = (((1,), (1,)), ((), ()))
@@ -36,15 +37,16 @@
     prev, nxt = jnp.maximum(t - 1, 0), jnp.minimum(t + 1, n - 1)
 
     loads = [
-        pltpu.make_async_copy(q_ref, query2, load_sem.at[3]),
-        pltpu.make_async_copy(new_ref, fresh_kv, load_sem.at[4]),
+        pltpu.make_async_copy(q_ref, query2, load_sem.at[6]),
+        pltpu.make_async_copy(new_ref, fresh_kv, load_sem.at[7]),
         pltpu.make_async_copy(cache_ref.at[0], kv.at[0], load_sem.at[0]),
         pltpu.make_async_copy(cache_ref.at[1], kv.at[1], load_sem.at[1]),
-        pltpu.make_async_copy(w_hbm, weight, load_sem.at[2]),
+    ] + [
+        pltpu.make_async_copy(w_hbm.at[:, piece], weight.at[:, piece], load_sem.at[2 + j])
+        for j, piece in enumerate((
+            pl.ds(half, WIDE), pl.ds(0, WIDE),
+            pl.ds(half + WIDE, half - WIDE), pl.ds(WIDE, half - WIDE)))
     ]
-    for load in loads:
-        load.start()
-
     barrier = pltpu.get_barrier_semaphore()
 
     @pl.when(has_prev)
@@ -54,6 +56,9 @@
     @pl.when(has_next)
     def _():
         pl.semaphore_signal(barrier, inc=1, device_id={"tp": nxt}, device_id_type=MESH)
+
+    for load in loads:
+        load.start()
 
     factor = HD ** -0.5 * math.log2(math.e)
     length = prefix_ref[0]
@@ -177,17 +182,33 @@
                 result_copy(d, i).start()
 
             out_ref[tokens(i), columns(d, i)] = results[d, i]
+            sum_copy(d, i).wait_send()
+
+        @pl.when(jnp.logical_not(is_first[d]) & (i >= BEHIND))
+        def _():
+            result_copy(d, i - BEHIND).wait_send()
 
     for part in range(PARTS):
         attend(part)
         if part == 0:
             loads[4].wait()
+            loads[5].wait()
+            for d in range(2):
+                @pl.when(is_first[d])
+                def _():
+                    stage[d, 0] = product(d, 0).astype(jnp.bfloat16)
             pl.semaphore_wait(barrier, has_prev.astype(jnp.int32) + has_next.astype(jnp.int32))
+            for d in range(2):
+                @pl.when(is_first[d])
+                def _():
+                    sum_copy(d, 0).start()
+            loads[6].wait()
+            loads[7].wait()
         if part < PARTS - 1:
             for d in range(2):
                 @pl.when(is_first[d])
                 def _():
-                    @pl.loop(part * per_part, (part + 1) * per_part)
+                    @pl.loop(max(part * per_part, 1), (part + 1) * per_part)
                     def _(i):
                         stage[d, i] = product(d, i).astype(jnp.bfloat16)
                         sum_copy(d, i).start()
@@ -210,13 +231,9 @@
                 def _():
                     work(d, i)
 
-    @pl.loop(0, count)
+    @pl.loop(count - min(BEHIND, count), count)
     def _(i):
         for d in range(2):
-            @pl.when(jnp.logical_not(is_owner[d]))
-            def _():
-                sum_copy(d, i).wait_send()
-
             @pl.when(jnp.logical_not(is_first[d]))
             def _():
                 result_copy(d, i).wait_send()
@@ -246,7 +263,7 @@
             pltpu.VMEM((2, count, deep, WIDE), jnp.bfloat16),
             pltpu.VMEM((2, count, deep, WIDE), jnp.bfloat16),
             pltpu.VMEM((2, count, deep, WIDE), jnp.bfloat16),
-            pltpu.SemaphoreType.DMA((5,)),
+            pltpu.SemaphoreType.DMA((8,)),
             pltpu.SemaphoreType.DMA((2, count)),
             pltpu.SemaphoreType.DMA((2, count)),
             pltpu.SemaphoreType.DMA((2, count)),

time: 38.6 us -> 38.6 us (level)
  no operation moved by 1% of the time
where the time goes in v5:
time: 38.6 us; the launch traced here: 38.4 us
  Pallas kernels  36.8 us (95%)
  local copies, waits for them, and re-layouts  0.97 us (3%)
  between operations  0.66 us (2%)
    pallas_call x1, Pallas kernels, per_device(): pl.pallas_call(functools.partial(kernel, n), out_shape=pltpu.VMEM((CH, dw...  36.8 us
    unnamed x1, local copies, waits for them, and re-layouts  0.97 us

profile of v5, /device:TPU:0, one launch (start us, length us, event | category | flops | bytes accessed | tf_op | source)
XLA Modules:
  0.0 38.4 jit_solution(7896367917994725182)
XLA Ops:
  0.7 36.8 %shard_map.55 = bf16[128,4096]{1,0:T(8,128)(2,1)S(1)} custom-call(bf16[128,256]{1,0:T(8,128)(2,1)} %bitcast.6, bf16[2,3584,128]{2,1,0:T(8,128)(2,1)} %bitcast.5, bf16[2,128,128]{2,1,0:T(8,128)(2,1)} %bitcast.7, bf16[256,4096]{1,0:T(8,128)(2,1)} %w_hbm.1, s32[1]{0:T(128)S(6)} %copy.8.prefix_ref), custom_call_target="tpu_custom_call" | custom-call | tf_op jit(solution)/shard_map/pallas_call | solution.py:250
  37.4 1.0 %copy.7 = bf16[1,128,4096]{2,1,0:T(8,128)(2,1)} copy(bf16[1,128,4096]{2,1,0:T(8,128)(2,1)S(1)} %bitcast.4) | data formatting | bytes 2097152

commit v6 on v5

--- a/solution.py
+++ b/solution.py
@@ -13,8 +13,8 @@
 CH = 128
 SAFE = 896
 TILE = 512
-WIDE = 256
-PARTS = 2
+WIDE = 512
+PARTS = 4
 SKEW = 5
 BEHIND = 4
 MASKED = -1e30

time: 38.6 us -> 38.4 us (level)
  no operation moved by 1% of the time
where the time goes in v6:
time: 38.4 us; the launch traced here: 38.3 us
  Pallas kernels  36.7 us (96%)
  local copies, waits for them, and re-layouts  0.97 us (3%)
  between operations  0.66 us (2%)
    pallas_call x1, Pallas kernels, per_device(): pl.pallas_call(functools.partial(kernel, n), out_shape=pltpu.VMEM((CH, dw...  36.7 us
    unnamed x1, local copies, waits for them, and re-layouts  0.97 us

profile of v6, /device:TPU:0, one launch (start us, length us, event | category | flops | bytes accessed | tf_op | source)
XLA Modules:
  0.0 38.3 jit_solution(5530932270116493696)
XLA Ops:
  0.7 36.7 %shard_map.55 = bf16[128,4096]{1,0:T(8,128)(2,1)S(1)} custom-call(bf16[128,256]{1,0:T(8,128)(2,1)} %bitcast.6, bf16[2,3584,128]{2,1,0:T(8,128)(2,1)} %bitcast.5, bf16[2,128,128]{2,1,0:T(8,128)(2,1)} %bitcast.7, bf16[256,4096]{1,0:T(8,128)(2,1)} %w_hbm.1, s32[1]{0:T(128)S(6)} %copy.8.prefix_ref), custom_call_target="tpu_custom_call" | custom-call | tf_op jit(solution)/shard_map/pallas_call | solution.py:250
  37.3 1.0 %copy.7 = bf16[1,128,4096]{2,1,0:T(8,128)(2,1)} copy(bf16[1,128,4096]{2,1,0:T(8,128)(2,1)S(1)} %bitcast.4) | data formatting | bytes 2097152

commit v7 on v6

--- a/solution.py
+++ b/solution.py
@@ -12,7 +12,7 @@
 HQ_DEV = 2
 CH = 128
 SAFE = 896
-TILE = 512
+TILE = 896
 WIDE = 512
 PARTS = 4
 SKEW = 5

time: 38.4 us -> 38.5 us (level)
  no operation moved by 1% of the time
where the time goes in v7:
time: 38.5 us; the launch traced here: 38.3 us
  Pallas kernels  36.7 us (95%)
  local copies, waits for them, and re-layouts  0.97 us (3%)
  between operations  0.66 us (2%)
    pallas_call x1, Pallas kernels, per_device(): pl.pallas_call(functools.partial(kernel, n), out_shape=pltpu.VMEM((CH, dw...  36.7 us
    unnamed x1, local copies, waits for them, and re-layouts  0.97 us

profile of v7, /device:TPU:0, one launch (start us, length us, event | category | flops | bytes accessed | tf_op | source)
XLA Modules:
  0.0 38.3 jit_solution(445516888578886524)
XLA Ops:
  0.7 36.7 %shard_map.55 = bf16[128,4096]{1,0:T(8,128)(2,1)S(1)} custom-call(bf16[128,256]{1,0:T(8,128)(2,1)} %bitcast.6, bf16[2,3584,128]{2,1,0:T(8,128)(2,1)} %bitcast.5, bf16[2,128,128]{2,1,0:T(8,128)(2,1)} %bitcast.7, bf16[256,4096]{1,0:T(8,128)(2,1)} %w_hbm.1, s32[1]{0:T(128)S(6)} %copy.8.prefix_ref), custom_call_target="tpu_custom_call" | custom-call | tf_op jit(solution)/shard_map/pallas_call | solution.py:250
  37.3 1.0 %copy.7 = bf16[1,128,4096]{2,1,0:T(8,128)(2,1)} copy(bf16[1,128,4096]{2,1,0:T(8,128)(2,1)S(1)} %bitcast.4) | data formatting | bytes 2097152
